TPU v7x, 32 devices: a whole 2x2x4 slice. The times are simulated.
32 devices in a mesh: box: 8 (over y, x, core), dir: 4 (over z).
Axes of the slice: x: 2, y: 2, z: 4, core: 2. Of those that a mesh axis runs over, the one named last changes fastest.
Arguments:
- child_field: float32 [2, 4, 256, 4608], P(None, None, 'box', 'dir'), may hold values from -6 to 6
- child_of: int32 [64, 4], P('box'), may hold values from 0 to 255, as said below
- shift_angle: float32 [4, 18432], P(None, 'dir'), may hold values from -3.140625 to 3.140625
- interp_index: int32 [6, 18432], P(None, 'dir'), may hold values from 0 to 4607, as said below
- interp_weight: float32 [6, 18432], P(None, 'dir'), may hold values from -0.2 to 0.5
- interaction_list: int32 [27, 64], replicated, may hold values from 0 to 63
- translation: float32 [2, 27, 18432], P(None, None, 'dir'), may hold values from -0.875 to 0.875
Outputs:
- child_incoming: float32 [2, 4, 256, 4608], P(None, None, 'box', 'dir')
Inputs may be any that keep to these rules, and one draw needn't show every extreme that they name: child_of lists every child box once; the parents p with p // 8 = q have exactly the children q * 32 to (q + 1) * 32 - 1. interp_index[j, k] differs from k // 4 by at most 8, and for j = 0 by exactly 8 where k // 4 lies 8 or more from both ends.
All inputs are finite; a program needn't handle non-finite values.
Results may differ from a plain program's by a relative error of at most 0.00007.
Values sent between devices are 32-bit elements; how exact they have to be, the bound alone decides.
A program may use at most 64 MiB of HBM per device.

v0:
```python
import jax
import jax.numpy as jnp
from jax import lax
from jax.sharding import PartitionSpec as P

KIDS = 4
HW = 8


def padded(block, sides, width):
    for axis, dim in sides:
        count = lax.axis_size(axis)
        forward = [(i, i + 1) for i in range(count - 1)]
        backward = [(target, source) for source, target in forward]
        low = lax.ppermute(
            lax.slice_in_dim(block, block.shape[dim] - width, None, axis=dim), axis, forward
        )
        high = lax.ppermute(lax.slice_in_dim(block, 0, width, axis=dim), axis, backward)
        block = jnp.concatenate([low, block, high], axis=dim)
    return block


def from_behind(block, axis, distance):
    devices = range(lax.axis_size(axis))
    route = [(i - distance, i) for i in devices if i - distance in devices]
    return lax.ppermute(block, axis, route)


def translate(source_field, interaction_list, table):

    def add_term(term, carry):
        source_ids = lax.dynamic_index_in_dim(interaction_list, term, 0, keepdims=False)
        source = jnp.take(source_field, source_ids, axis=0)
        op_real = lax.dynamic_index_in_dim(table[0], term, 0, keepdims=False)
        op_imag = lax.dynamic_index_in_dim(table[1], term, 0, keepdims=False)
        src_real = source[:, 0]
        src_imag = source[:, 1]
        return (
            carry[0] + op_real * src_real - op_imag * src_imag,
            carry[1] + op_real * src_imag + op_imag * src_real,
        )

    start = jnp.zeros(source_field[:, 0].shape, jnp.float32)
    real_sum, imag_sum = lax.fori_loop(0, interaction_list.shape[0], add_term, (start, start))
    return jnp.stack([real_sum, imag_sum], axis=1)


def shards(
    child_field, child_of, shift_angle, interp_index, interp_weight, interaction_list, translation
):
    box_count = lax.axis_size("box")
    box_index = lax.axis_index("box")
    dir_index = lax.axis_index("dir")
    halves, fields, own_boxes, strip_child = child_field.shape
    parents = child_of.shape[0]
    strip_par = interp_index.shape[1]
    dir_piece = strip_par // box_count
    block_len = 512
    block_count = strip_par // block_len
    window = block_len // 4 + 2 * HW
    row_count = halves * fields * own_boxes

    def build_matrix(block_at):
        index_block = lax.dynamic_slice_in_dim(interp_index, block_at * block_len, block_len, 1)
        weight_block = lax.dynamic_slice_in_dim(interp_weight, block_at * block_len, block_len, 1)
        columns = index_block - dir_index * strip_child + HW - block_at * (block_len // 4)
        places = lax.iota(jnp.int32, window)[:, None]
        matrix = jnp.zeros((window, block_len), jnp.float32)
        for stencil_at in range(index_block.shape[0]):
            matrix = matrix + jnp.where(
                columns[stencil_at][None, :] == places, weight_block[stencil_at][None, :], 0.0
            )
        return matrix

    matrices = lax.map(build_matrix, jnp.arange(block_count, dtype=jnp.int32))
    extended = padded(child_field, (("dir", 3),), HW)
    flattened = extended.reshape(row_count, strip_child + 2 * HW)

    def interp_block(block_at, summed):
        columns = lax.dynamic_slice_in_dim(flattened, block_at * (block_len // 4), window, 1)
        product = jnp.dot(
            columns,
            matrices[block_at],
            precision=lax.Precision.HIGHEST,
            preferred_element_type=jnp.float32,
        )
        return lax.dynamic_update_slice_in_dim(summed, product, block_at * block_len, 1)

    interpolated = lax.fori_loop(
        0, block_count, interp_block, jnp.zeros((row_count, strip_par), jnp.float32)
    )
    interpolated = interpolated.reshape(halves, fields, own_boxes, strip_par)
    local_kids = (child_of - box_index * own_boxes).reshape(-1)
    selector = (local_kids[:, None] == lax.iota(jnp.int32, own_boxes)[None, :]).astype(jnp.float32)
    picked = jnp.einsum(
        "qb,crbn->qcrn",
        selector,
        interpolated,
        precision=lax.Precision.HIGHEST,
        preferred_element_type=jnp.float32,
    )
    picked = picked.reshape(parents, KIDS, halves, fields, strip_par)
    cosines = jnp.cos(shift_angle)[None, :, None, :]
    sine_part = jnp.sin(shift_angle)[None, :, None, :]
    agg_real = jnp.sum(picked[:, :, 0] * cosines - picked[:, :, 1] * sine_part, axis=1)
    agg_imag = jnp.sum(picked[:, :, 0] * sine_part + picked[:, :, 1] * cosines, axis=1)
    aggregated = jnp.stack([agg_real, agg_imag], axis=1)
    outbound = aggregated.reshape(parents, halves, fields, box_count, dir_piece)
    table = lax.dynamic_slice_in_dim(translation, box_index * dir_piece, dir_piece, 2)
    received = lax.all_to_all(outbound, "box", split_axis=3, concat_axis=0, tiled=True)
    answered = translate(received[:, :, :, 0], interaction_list, table)
    incoming = lax.all_to_all(
        answered[:, :, :, None], "box", split_axis=0, concat_axis=3, tiled=True
    )
    incoming = incoming.reshape(parents, halves, fields, strip_par)
    in_real = incoming[:, 0][:, None]
    in_imag = incoming[:, 1][:, None]
    spread_real = in_real * cosines + in_imag * sine_part
    spread_imag = in_imag * cosines - in_real * sine_part
    spread_kids = jnp.stack([spread_real, spread_imag], axis=2).reshape(
        parents * KIDS, halves, fields, strip_par
    )
    spread = jnp.einsum(
        "qb,qcrn->crbn",
        selector,
        spread_kids,
        precision=lax.Precision.HIGHEST,
        preferred_element_type=jnp.float32,
    ).reshape(row_count, strip_par)

    def anterp_block(block_at, summed):
        columns = lax.dynamic_slice_in_dim(spread, block_at * block_len, block_len, 1)
        product = jnp.dot(
            columns,
            matrices[block_at].T,
            precision=lax.Precision.HIGHEST,
            preferred_element_type=jnp.float32,
        )
        current = lax.dynamic_slice_in_dim(summed, block_at * (block_len // 4), window, 1)
        return lax.dynamic_update_slice_in_dim(
            summed, current + product, block_at * (block_len // 4), 1
        )

    widened = lax.fori_loop(
        0, block_count, anterp_block, jnp.zeros((row_count, strip_child + 2 * HW), jnp.float32)
    )
    widened = widened.reshape(halves, fields, own_boxes, strip_child + 2 * HW)
    inner = widened[..., HW : HW + strip_child]
    from_below = from_behind(widened[..., strip_child + HW :], "dir", 1)
    from_above = from_behind(widened[..., :HW], "dir", -1)
    return inner.at[..., :HW].add(from_below).at[..., strip_child - HW :].add(from_above)


def solution(mesh):
    in_specs = (
        P(None, None, "box", "dir"),
        P("box", None),
        P(None, "dir"),
        P(None, "dir"),
        P(None, "dir"),
        P(),
        P(None, None, "dir"),
    )
    out_specs = P(None, None, "box", "dir")
    return jax.shard_map(shards, mesh=mesh, in_specs=in_specs, out_specs=out_specs, check_vma=False)
```

profile of v0, /device:TPU:0, one launch (start us, length us, event | category | flops | bytes accessed | tf_op | source)
XLA Modules:
  0.0 434.7 jit_solution(3527944600796394326)
XLA Ops:
  1.2 4.9 %collective-permute-start = (f32[2,4,32,8]{3,2,1,0:T(8,128)S(1)}, f32[2,4,32,8]{3,2,1,0:T(8,128)S(1)}, u32[]{:S(2)}, u32[]{:S(2)}) collective-permute-start(f32[2,4,32,8]{3,2,1,0:T(8,128)S(1)} %get-tuple-element.474), channel_id=1, source_target_pairs={{0,1},{1,2},{2,3},{4,5},{5,6},{6,7},{8,9},{9,10},{10,11},{12,13},{... | collective-permute-start | bytes 24584 | tf_op jit(solution)/shard_map/ppermute | solution.py:15
  7.5 42.3 %while.56 = (s32[]{:T(128)}, f32[9,144,512]{2,1,0:T(8,128)}, s32[9]{0:T(128)S(1)}, s32[6,4608]{1,0:T(8,128)}, s32[]{:T(128)}, /*index=5*/f32[6,4608]{1,0:T(8,128...) while((s32[]{:T(128)}, f32[9,144,512]{2,1,0:T(8,128)}, ...), condition=%wide.region_1.2_spmd, body=%wide.region_0.1_spmd.sunk | while | flops 1262604 | bytes 394043 | solution.py:75
  56.8 21.4 %while.57 = (s32[]{:T(128)}, f32[256,4608]{1,0:T(8,128)}, f32[256,1168]{1,0:T(8,128)S(1)}, f32[9,144,512]{2,1,0:T(8,128)}, s32[]{:T(128)}, /*index=5*/s32[]{:T(128)}, s32[]{:T(128)}, s32[]{:T(128)}, s32[]{:T(128)}, s32[]{:T(128)}) while((s32[]{:T(128)}, f32[256,4608]{1,0:T(8,128)}, f32[256,1168]{1,0:T(8,128)S(1)}, f32[9,144,512]{2,1,0:T(8,128)}, ...), condition=%wide.region_3.4_spmd, body=%wide.region_2.3_spmd.sunk | while | flops 226492432 | bytes 1082057 | solution.py:89
  78.2 4.8 %fusion.17 = f32[8,4,2,4,4608]{4,0,3,2,1:T(8,128)S(1)} fusion(f32[2,4,32,4608,1]{3,2,1,0,4:T(8,128)} %bitcast.150, s32[8,4]{0,1:T(4,128)S(1)} %broadcast_subtract_fusion), kind=kOutput, calls=%fused_computation.57 | convolution fusion | flops 452985856 | bytes 9437312 | tf_op jit(solution)/shard_map/qb,crbn->qcrn/dot_general | solution.py:95
  85.6 3.7 all-to-all-start
  89.6 18.0 %all-to-all-done = f32[8,2,4,8,576]{4,0,2,1,3:T(8,128)S(1)} async-done(((f32[8,2,4,8,576]{4,0,2,1,3:T(8,128)}), f32[8,2,4,8,576]{4,0,2,1,3:T(8,128)S(1)}, u32[]{:S(2)}, u32[]{:S(2)}) %all-to-all-start) | async-done | bytes 1179680 | tf_op jit(solution)/shard_map/all_to_all | solution.py:110
  109.6 249.6 %while.59 = (s32[]{:T(128)}, f32[64,4,576]{2,1,0:T(4,128)S(1)}, f32[64,4,576]{2,1,0:T(4,128)}, f32[2,27,576]{2,1,0:T(8,128)S(1)}, s32[27,64]{1,0:T(8,128)}, /*index=5*/f32[64,2,4,576]{3,2,1,0:T(4,128)}, s32[]{:T(128)}, s32[]{:T(128)}) while((s32[]{:T(128)}, f32[64,4,576]{2,1,0:T(4,128)S(1)}, f32[64,4,576]{2,1,0:T(4,128)}, ...), condition=%wide.region_7.8_spmd.clone, body=%wide.region_6.7_spmd.clone.sunk | while | flops 1771075 | bytes 8525803 | solution.py:44
  110.3 3.7 gather_fusion
  127.8 3.7 gather_fusion
  155.6 3.7 gather_fusion
  174.2 3.7 gather_fusion
  202.0 3.7 gather_fusion
  211.3 3.7 gather_fusion
  220.6 3.7 gather_fusion
  257.7 3.7 gather_fusion
  285.6 3.7 gather_fusion
  304.2 3.7 gather_fusion
  313.4 3.7 gather_fusion
  332.0 3.7 gather_fusion
  361.7 3.7 all-to-all-start.1
  367.9 15.5 %all-to-all-done.1 = f32[64,2,4,1,576]{4,2,1,3,0:T(4,128)S(1)} async-done(((f32[64,2,4,1,576]{4,2,1,3,0:T(4,128)}), f32[64,2,4,1,576]{4,2,1,3,0:T(4,128)S(1)}, u32[]{:S(2)}, u32[]{:S(2)}) %all-to-all-start.1) | async-done | bytes 1179680 | tf_op jit(solution)/shard_map/all_to_all | solution.py:112
  396.7 4.8 %fusion.12 = f32[2,4,4608,32]{2,3,1,0:T(8,128)} fusion(f32[32,1,4,4608]{3,0,2,1:T(8,128)S(1)} %get-tuple-element.468, f32[32,1,4,4608]{3,0,2,1:T(8,128)S(1)} %get-tuple-element.467, s32[32]{0:T(128)S(1)} %eq.185), kind=kOutput, calls=%fused_computation.36 | convolution fusion | flops 454165504 | bytes 9437312 | tf_op jit(solution)/shard_map/qb,qcrn->crbn/dot_general | solution.py:123
  401.6 16.5 %while.58 = (s32[]{:T(128)}, f32[256,1168]{0,1:T(8,128)S(1)}, f32[256,4608]{1,0:T(8,128)}, f32[9,144,512]{2,1,0:T(8,128)}, s32[]{:T(128)}, /*index=5*/s32[]{:T(128)}, s32[]{:T(128)}, s32[]{:T(128)}, s32[]{:T(128)}, s32[]{:T(128)}) while((s32[]{:T(128)}, f32[256,1168]{0,1:T(8,128)S(1)}, f32[256,4608]{1,0:T(8,128)}, f32[9,144,512]{2,1,0:T(8,128)}, ...), condition=%wide.region_9.10_spmd, body=%wide.region_8.9_spmd.sunk | while | flops 226529296 | bytes 1114825 | solution.py:144
  419.2 4.5 %collective-permute-start.2 = (f32[2,4,32,8]{3,2,1,0:T(8,128)S(1)}, f32[2,4,32,8]{3,2,1,0:T(8,128)S(1)}, u32[]{:S(2)}, u32[]{:S(2)}) collective-permute-start(f32[2,4,32,8]{3,2,1,0:T(8,128)S(1)} %get-tuple-element.470), channel_id=1, source_target_pairs={{0,1},{1,2},{2,3},{4,5},{5,6},{6,7},{8,9},{9,10},{10,11},{12,13},{... | collective-permute-start | bytes 24584 | tf_op jit(solution)/shard_map/ppermute | solution.py:26
  (328 shorter events, 317.0 us)
Async XLA Ops:
  0.0 89.3 %copy-start = (f32[2,27,4608]{2,0,1:T(2,128)S(1)}, f32[2,27,4608]{2,0,1:T(2,128)}, u32[]{:S(2)}) copy-start(f32[2,27,4608]{2,0,1:T(2,128)} %param.25) | copy-start | bytes 2985988
  0.0 52.5 %copy-start.1 = (f32[2,4,32,1152]{3,2,1,0:T(8,128)S(1)}, f32[2,4,32,1152]{3,2,1,0:T(8,128)}, u32[]{:S(2)}) copy-start(f32[2,4,32,1152]{3,2,1,0:T(8,128)} %param.19) | copy-start | bytes 3538948
  0.0 51.8 %copy-start.6 = (s32[8,4]{0,1:T(4,128)S(1)}, s32[8,4]{0,1:T(4,128)}, u32[]{:S(2)}) copy-start(s32[8,4]{0,1:T(4,128)} %param.20) | copy-start | bytes 388
  1.2 50.6 %collective-permute-start = (f32[2,4,32,8]{3,2,1,0:T(8,128)S(1)}, f32[2,4,32,8]{3,2,1,0:T(8,128)S(1)}, u32[]{:S(2)}, u32[]{:S(2)}) collective-permute-start(f32[2,4,32,8]{3,2,1,0:T(8,128)S(1)} %get-tuple-element.474), channel_id=1, source_target_pairs={{0,1},{1,2},{2,3},{4,5},{5,6},{6,7},{8,9},{9,10},{10,11},{12,13},{... | collective-permute-start | bytes 24584 | tf_op jit(solution)/shard_map/ppermute | solution.py:15
  6.2 46.3 %collective-permute-start.1 = (f32[2,4,32,8]{3,2,1,0:T(8,128)S(1)}, f32[2,4,32,8]{3,2,1,0:T(8,128)}, u32[]{:S(2)}, u32[]{:S(2)}) collective-permute-start(f32[2,4,32,8]{3,2,1,0:T(8,128)S(1)} %get-tuple-element.473), channel_id=1, source_target_pairs={{1,0},{2,1},{3,2},{5,4},{6,5},{7,6},{9,8},{10,9},{11,10},{13,12},{... | collective-permute-start | bytes 24584 | tf_op jit(solution)/shard_map/ppermute | solution.py:18
  51.9 0.7 copy-start.5
  78.2 4.8 %copy-start.3 = (f32[4,4608]{1,0:T(4,128)S(1)}, f32[4,4608]{1,0:T(4,128)}, u32[]{:S(2)}) copy-start(f32[4,4608]{1,0:T(4,128)} %get-tuple-element.476) | copy-start | bytes 221188
  78.2 4.8 %copy-start.4 = (f32[4,4608]{1,0:T(4,128)S(1)}, f32[4,4608]{1,0:T(4,128)}, u32[]{:S(2)}) copy-start(f32[4,4608]{1,0:T(4,128)} %get-tuple-element.475) | copy-start | bytes 221188
  85.6 21.9 %all-to-all-start = ((f32[8,2,4,8,576]{4,0,2,1,3:T(8,128)}), f32[8,2,4,8,576]{4,0,2,1,3:T(8,128)S(1)}, u32[]{:S(2)}, u32[]{:S(2)}) async-start(f32[8,2,4,8,576]{4,0,2,1,3:T(8,128)} %copy.29), calls=%async_computation | async-start | bytes 2621440 | tf_op jit(solution)/shard_map/all_to_all | solution.py:110
  361.7 21.7 %all-to-all-start.1 = ((f32[64,2,4,1,576]{4,2,1,3,0:T(4,128)}), f32[64,2,4,1,576]{4,2,1,3,0:T(4,128)S(1)}, u32[]{:S(2)}, u32[]{:S(2)}) async-start(f32[64,2,4,1,576]{4,2,1,3,0:T(4,128)} %maximum_bitcast_fusion), calls=%async_computation.1 | async-start | bytes 2621440 | tf_op jit(solution)/shard_map/all_to_all | solution.py:112
  419.2 7.0 %collective-permute-start.2 = (f32[2,4,32,8]{3,2,1,0:T(8,128)S(1)}, f32[2,4,32,8]{3,2,1,0:T(8,128)S(1)}, u32[]{:S(2)}, u32[]{:S(2)}) collective-permute-start(f32[2,4,32,8]{3,2,1,0:T(8,128)S(1)} %get-tuple-element.470), channel_id=1, source_target_pairs={{0,1},{1,2},{2,3},{4,5},{5,6},{6,7},{8,9},{9,10},{10,11},{12,13},{... | collective-permute-start | bytes 24584 | tf_op jit(solution)/shard_map/ppermute | solution.py:26
  424.1 7.2 %collective-permute-start.3 = (f32[2,4,32,8]{3,2,1,0:T(8,128)}, f32[2,4,32,8]{3,2,1,0:T(8,128)}, u32[]{:S(2)}, u32[]{:S(2)}) collective-permute-start(f32[2,4,32,8]{3,2,1,0:T(8,128)} %get-tuple-element.469), channel_id=1, source_target_pairs={{1,0},{2,1},{3,2},{5,4},{6,5},{7,6},{9,8},{10,9},{11,10},{13,12},{... | collective-permute-start | bytes 24584 | tf_op jit(solution)/shard_map/ppermute | solution.py:26
  428.2 4.2 copy-start.2
where the time goes:
time: 442 us; the launch traced here: 435 us
  other arithmetic  172 us (39%)
  local copies, waits for them, and re-layouts  145 us (33%)
  matrix products  47.3 us (11%)
  waiting for transfers between devices  37.5 us (8%)
  starting transfers between devices  19.5 us (4%)
  loops' own time  13.3 us (3%)
    gather x27, local copies, waits for them, and re-layouts, add_term(): source = jnp.take(source_field, source_ids, axis=0)  98.8 us
    add x27, other arithmetic, add_term(): carry[1] + op_real * src_imag + op_imag * src_real  66.3 us
    select_n x54, other arithmetic, add_term(): source = jnp.take(source_field, source_ids, axis=0)  63.5 us
    dot_general x9, matrix products, interp_block(): jnp.dot(columns, matrices[block_at], precision=lax.Precision.HIGHEST, pre...  21.4 us
    and x27, other arithmetic, add_term(): source = jnp.take(source_field, source_ids, axis=0)  18.8 us
    all_to_all x1, waiting for transfers between devices, shards(): lax.all_to_all(outbound, 'box', split_axis=3, concat_axis=0, tiled=True)  18 us
    dot_general x9, matrix products, anterp_block(): jnp.dot(columns, matrices[block_at].T, precision=lax.Precision.HIGHEST, p...  16.3 us
    all_to_all x1, waiting for transfers between devices, shards(): lax.all_to_all(answered[:, :, :, None], 'box', split_axis=0, concat_axis=...  15.5 us
  transfers between devices with their start and end apart: 6, of which 4 were waited for; matrix products, arithmetic and copies ran while one was open for 9% of the time, Pallas kernels for 0%

commit v1 on v0

v1 whole, which is shorter than its diff:
```python
import jax
import jax.numpy as jnp
from jax import lax
from jax.experimental import pallas as pl
from jax.experimental.pallas import tpu as pltpu
from jax.sharding import PartitionSpec as P

HW = 8
LANES = 128
RATIO = 4
BAND = LANES // RATIO + 2 * HW
WINDOW = 2 * LANES
VMEM = pl.BlockSpec(memory_space=pltpu.VMEM)
SMEM = pl.BlockSpec(memory_space=pltpu.SMEM)


def rotated(value):
    half = value.shape[0] // 2
    sign = jnp.where(lax.broadcasted_iota(jnp.int32, value.shape, 0) < half, -1.0, 1.0)
    return pltpu.roll(value, half, 0) * sign


def split(value):
    high = value.astype(jnp.bfloat16)
    low = (value - high.astype(jnp.float32)).astype(jnp.bfloat16)
    return high, low


def lanes_of(chunk):
    return pl.ds(pl.multiple_of(chunk * LANES, LANES), LANES)


def band_of(chunk, first_child, index_ref, weight_ref):
    place = lax.broadcasted_iota(jnp.int32, (BAND, LANES), 0)
    base = first_child + chunk * (LANES // RATIO) - HW
    band = jnp.zeros((BAND, LANES), jnp.float32)
    for stencil_at in range(index_ref.shape[0]):
        row = index_ref[stencil_at : stencil_at + 1, lanes_of(chunk)] - base
        weight = weight_ref[stencil_at : stencil_at + 1, lanes_of(chunk)]
        band = band + jnp.where(row == place, weight, 0.0)
    return band


def band_rows(corner):
    return pl.ds(pl.multiple_of(corner * (LANES // RATIO), LANES // RATIO), BAND)


def aggregate_kernel(x_ref, cos_ref, sin_ref, index_ref, weight_ref, kids_ref, out_ref,
                     high_ref, low_ref, matrix_ref, field_ref):
    first_child = lax.axis_index("dir") * (index_ref.shape[1] // RATIO)
    high, low = split(x_ref[...])
    high_ref[...] = high
    low_ref[...] = low
    matrix_ref[...] = jnp.zeros_like(matrix_ref)
    parents, kids = kids_ref.shape

    def one(chunk, carry):
        corner = lax.rem(chunk, RATIO)
        columns = pl.ds(pl.multiple_of(chunk // RATIO * LANES, LANES), WINDOW)
        band_high, band_low = split(band_of(chunk, first_child, index_ref, weight_ref))
        matrix_ref[corner, band_rows(corner), :LANES] = band_high
        matrix_ref[corner, band_rows(corner), LANES:] = band_low
        both = jnp.dot(high_ref[:, columns], matrix_ref[corner],
                       preferred_element_type=jnp.float32)
        rest = jnp.dot(low_ref[:, columns], matrix_ref[corner, :, :LANES],
                       preferred_element_type=jnp.float32)
        field_ref[...] = (both[:, :LANES] + (both[:, LANES:] + rest)).reshape(field_ref.shape)
        cosines = cos_ref[:, lanes_of(chunk)]
        sines = sin_ref[:, lanes_of(chunk)]
        for parent in range(parents):
            straight = turned = 0.0
            for kid in range(kids):
                value = field_ref[kids_ref[parent, kid]]
                straight = straight + cosines[kid : kid + 1] * value
                turned = turned + sines[kid : kid + 1] * value
            out_ref[chunk, parent] = straight + rotated(turned)
        return carry

    lax.fori_loop(0, index_ref.shape[1] // LANES, one, 0)


def spread_kernel(in_ref, cos_ref, sin_ref, index_ref, weight_ref, slot_ref, out_ref,
                  twice_ref, low_ref, values_ref, phase_ref):
    first_child = lax.axis_index("dir") * (index_ref.shape[1] // RATIO)
    twice_ref[...] = jnp.zeros_like(twice_ref)
    low_ref[...] = jnp.zeros_like(low_ref)
    out_ref[...] = jnp.zeros_like(out_ref)
    boxes = slot_ref.shape[0]
    kids = cos_ref.shape[0]
    rows = out_ref.shape[0] // boxes

    def one(chunk, carry):
        corner = lax.rem(chunk, RATIO)
        columns = pl.ds(pl.multiple_of(chunk // RATIO * LANES, LANES), WINDOW)
        band_high, band_low = split(band_of(chunk, first_child, index_ref, weight_ref))
        twice_ref[corner, band_rows(corner), :LANES] = band_high
        twice_ref[corner, band_rows(corner), LANES:] = band_high
        low_ref[corner, band_rows(corner), :] = band_low
        for kid in range(kids):
            for half, table_ref in enumerate((cos_ref, sin_ref)):
                phase_ref[half, kid] = jnp.broadcast_to(
                    table_ref[kid : kid + 1, lanes_of(chunk)], phase_ref.shape[2:])
        for box in range(boxes):
            slot = slot_ref[box]
            value = in_ref[chunk, slot // kids]
            kid = lax.rem(slot, kids)
            cosine, sine = phase_ref[0, kid], phase_ref[1, kid]
            values_ref[box * rows : (box + 1) * rows, :] = cosine * value - sine * rotated(value)
        high, low = split(values_ref[...])
        dims = (((1,), (1,)), ((), ()))
        product = lax.dot_general(jnp.concatenate([high, low], axis=1), twice_ref[corner], dims,
                                  preferred_element_type=jnp.float32)
        product = product + lax.dot_general(high, low_ref[corner], dims,
                                            preferred_element_type=jnp.float32)
        out_ref[:, columns] += product
        return carry

    lax.fori_loop(0, index_ref.shape[1] // LANES, one, 0)


def exchange_kernel(out_ref, list_ref, table_ref, back_ref, answer, operator,
                    sent, arrived, returned, home, near, *source):
    chunks, parents = out_ref.shape[:2]
    count = lax.axis_size("box")
    me = lax.axis_index("box")
    terms = list_ref.shape[0]
    rounds = len(source)

    def first(owner):
        return chunks * owner // count

    def held(owner):
        return first(owner + 1) - first(owner)

    def other(step):
        return lax.rem(me + step, count)

    def block(owner):
        return pl.ds(owner * parents, parents)

    barrier = pltpu.get_barrier_semaphore()

    def greet(step, carry):
        pl.semaphore_signal(barrier, inc=1, device_id={"box": other(step)},
                            device_id_type=pl.DeviceIdType.MESH)
        return carry

    lax.fori_loop(1, count, greet, 0)
    pl.semaphore_wait(barrier, count - 1)

    def outbound(owner, at):
        chunk = first(owner) + at
        return pltpu.make_async_remote_copy(
            src_ref=out_ref.at[chunk], dst_ref=source[at].at[block(me)],
            send_sem=sent.at[chunk], recv_sem=arrived.at[at, me],
            device_id={"box": owner}, device_id_type=pl.DeviceIdType.MESH)

    def inbound(owner, at):
        return pltpu.make_async_remote_copy(
            src_ref=out_ref.at[first(me) + at], dst_ref=source[at].at[block(owner)],
            send_sem=sent.at[first(me) + at], recv_sem=arrived.at[at, owner],
            device_id={"box": owner}, device_id_type=pl.DeviceIdType.MESH)

    def homebound(owner, at):
        return pltpu.make_async_remote_copy(
            src_ref=answer.at[at, block(owner)], dst_ref=back_ref.at[first(me) + at],
            send_sem=returned.at[at, owner], recv_sem=home.at[first(me) + at],
            device_id={"box": owner}, device_id_type=pl.DeviceIdType.MESH)

    def from_owner(owner, at):
        return pltpu.make_async_remote_copy(
            src_ref=answer.at[at, block(me)], dst_ref=back_ref.at[first(owner) + at],
            send_sem=returned.at[at, me], recv_sem=home.at[first(owner) + at],
            device_id={"box": owner}, device_id_type=pl.DeviceIdType.MESH)

    def own_out(at):
        return pltpu.make_async_copy(out_ref.at[first(me) + at], source[at].at[block(me)],
                                     near.at[at])

    def own_back(at):
        return pltpu.make_async_copy(answer.at[at, block(me)], back_ref.at[first(me) + at],
                                     near.at[at])

    def each(act):
        def step_of(step, carry):
            act(other(step))
            return carry

        lax.fori_loop(1, count, step_of, 0)

    for at in range(rounds):

        def send(owner):
            pl.when(at < held(owner))(lambda: outbound(owner, at).start())

        each(send)
        pl.when(at < held(me))(lambda: own_out(at).start())

    def translate_group(at, owner):
        unroll = 3 if terms % 3 == 0 else 1

        def some(term_at, carry):
            straight, turned = list(carry[0]), list(carry[1])
            for part in range(unroll):
                term = term_at * unroll + part
                op_real = operator[0, term]
                op_imag = operator[1, term]
                for parent in range(parents):
                    value = source[at][list_ref[term, owner * parents + parent]]
                    straight[parent] = straight[parent] + op_real * value
                    turned[parent] = turned[parent] + op_imag * value
            return tuple(straight), tuple(turned)

        zero = jnp.zeros(answer.shape[2:], jnp.float32)
        straight, turned = lax.fori_loop(
            0, terms // unroll, some, ((zero,) * parents, (zero,) * parents))
        for parent in range(parents):
            answer[at, owner * parents + parent] = straight[parent] + rotated(turned[parent])

    for at in range(rounds):

        @pl.when(at < held(me))
        def _():
            each(lambda owner: inbound(owner, at).wait_recv())
            own_out(at).wait()
            for half in range(2):
                for term in range(terms):
                    operator[half, term] = jnp.broadcast_to(
                        table_ref[half, term : term + 1, lanes_of(first(me) + at)],
                        operator.shape[2:])

            def reply(owner):
                translate_group(at, owner)
                homebound(owner, at).start()

            each(reply)
            translate_group(at, me)
            own_back(at).start()

    for at in range(rounds):

        def finish(owner):
            @pl.when(at < held(owner))
            def _():
                outbound(owner, at).wait_send()
                from_owner(owner, at).wait_recv()

        each(finish)

        @pl.when(at < held(me))
        def _():
            each(lambda owner: homebound(owner, at).wait_send())
            own_back(at).wait()


def shards(
    child_field, child_of, shift_angle, interp_index, interp_weight, interaction_list, translation
):
    box_count = lax.axis_size("box")
    box_index = lax.axis_index("box")
    dir_count = lax.axis_size("dir")
    halves, fields, own_boxes, strip_child = child_field.shape
    parents, kids = child_of.shape
    strip_par = interp_index.shape[1]
    chunks = strip_par // LANES
    parts = halves * fields
    rows = own_boxes * parts
    rounds = -(-chunks // box_count)
    width = strip_child + LANES
    f32, bf16 = jnp.float32, jnp.bfloat16
    limit = 48 * 1024 * 1024

    forward = [(i, i + 1) for i in range(dir_count - 1)]
    backward = [(i + 1, i) for i in range(dir_count - 1)]
    by_box = jnp.transpose(child_field, (2, 0, 1, 3)).reshape(rows, strip_child)
    low = lax.ppermute(by_box[:, strip_child - HW :], "dir", forward)
    high = lax.ppermute(by_box[:, :HW], "dir", backward)
    extended = jnp.concatenate(
        [low, by_box, high, jnp.zeros((rows, width - strip_child - 2 * HW), f32)], axis=1)
    cosines = jnp.cos(shift_angle)
    sines = jnp.sin(shift_angle)
    local = child_of - box_index * own_boxes
    slots = jnp.sum(
        jnp.where(local.reshape(-1)[:, None] == lax.iota(jnp.int32, own_boxes)[None, :],
                  lax.iota(jnp.int32, parents * kids)[:, None], 0), axis=0).astype(jnp.int32)

    outgoing = pl.pallas_call(
        aggregate_kernel,
        out_shape=jax.ShapeDtypeStruct((chunks, parents, parts, LANES), f32),
        in_specs=[VMEM] * 5 + [SMEM],
        out_specs=VMEM,
        scratch_shapes=[
            pltpu.VMEM((rows, width), bf16),
            pltpu.VMEM((rows, width), bf16),
            pltpu.VMEM((RATIO, WINDOW, 2 * LANES), bf16),
            pltpu.VMEM((own_boxes, parts, LANES), f32),
        ],
        compiler_params=pltpu.CompilerParams(vmem_limit_bytes=limit),
    )(extended, cosines, sines, interp_index, interp_weight, local)

    incoming = pl.pallas_call(
        exchange_kernel,
        out_shape=jax.ShapeDtypeStruct((chunks, parents, parts, LANES), f32),
        in_specs=[VMEM, SMEM, VMEM],
        out_specs=VMEM,
        scratch_shapes=[
            pltpu.VMEM((rounds, box_count * parents, parts, LANES), f32),
            pltpu.VMEM((2, interaction_list.shape[0], parts, LANES), f32),
            pltpu.SemaphoreType.DMA((chunks,)),
            pltpu.SemaphoreType.DMA((rounds, box_count)),
            pltpu.SemaphoreType.DMA((rounds, box_count)),
            pltpu.SemaphoreType.DMA((chunks,)),
            pltpu.SemaphoreType.DMA((rounds,)),
            *[pltpu.VMEM((box_count * parents, parts, LANES), f32)] * rounds,
        ],
        compiler_params=pltpu.CompilerParams(
            collective_id=0, has_side_effects=True, vmem_limit_bytes=limit),
    )(outgoing, interaction_list, translation)

    widened = pl.pallas_call(
        spread_kernel,
        out_shape=jax.ShapeDtypeStruct((rows, width), f32),
        in_specs=[VMEM] * 5 + [SMEM],
        out_specs=VMEM,
        scratch_shapes=[
            pltpu.VMEM((RATIO, WINDOW, 2 * LANES), bf16),
            pltpu.VMEM((RATIO, WINDOW, LANES), bf16),
            pltpu.VMEM((rows, LANES), f32),
            pltpu.VMEM((2, kids, parts, LANES), f32),
        ],
        compiler_params=pltpu.CompilerParams(vmem_limit_bytes=limit),
    )(incoming, cosines, sines, interp_index, interp_weight, slots)

    from_below = lax.ppermute(widened[:, strip_child + HW : strip_child + 2 * HW], "dir", forward)
    from_above = lax.ppermute(widened[:, :HW], "dir", backward)
    inner = widened[:, HW : HW + strip_child]
    inner = inner + jnp.pad(from_below, ((0, 0), (0, strip_child - HW)))
    inner = inner + jnp.pad(from_above, ((0, 0), (strip_child - HW, 0)))
    return jnp.transpose(inner.reshape(own_boxes, halves, fields, strip_child), (1, 2, 0, 3))


def solution(mesh):
    in_specs = (
        P(None, None, "box", "dir"),
        P("box", None),
        P(None, "dir"),
        P(None, "dir"),
        P(None, "dir"),
        P(),
        P(None, None, "dir"),
    )
    out_specs = P(None, None, "box", "dir")
    return jax.shard_map(shards, mesh=mesh, in_specs=in_specs, out_specs=out_specs, check_vma=False)
```

time: 442 us -> 89.5 us (0.20); the launches traced: 435 us -> 89.2 us
  other arithmetic: 172 us -> 0.5 us
  local copies, waits for them, and re-layouts: 145 us -> 7.83 us
  Pallas kernels: 0 us -> 60.5 us
  matrix products: 47.3 us -> 0 us
  waiting for transfers between devices: 37.5 us -> 6.9 us
  loops' own time: 13.3 us -> 0 us
  starting transfers between devices: 19.5 us -> 13.2 us
    gather x27 -> x0, local copies, waits for them, and re-layouts: 98.8 us -> none  [add_term(): source = jnp.take(source_field, source_ids, axis=0)]
    add x30 -> x1, other arithmetic: 71.3 us -> 0.4 us  [shards(): inner = inner + jnp.pad(from_above, ((0, 0), (strip_child - HW, 0)))]
    select_n x54 -> x0, other arithmetic: 63.5 us -> none  [add_term(): source = jnp.take(source_field, source_ids, axis=0)]
    pallas_call x0 -> x3, Pallas kernels: none -> 60.5 us  [the longest x1 36 us: shards(): pl.pallas_call(exchange_kernel, out_shape=jax.ShapeDtypeStruct((chunks, p...]
    dot_general x20 -> x0, matrix products: 47.3 us -> none  [the longest x9 21.4 us: interp_block(): jnp.dot(columns, matrices[block_at], precision=lax.Precision.HIGHEST, pre...]
    all_to_all x2 -> x0, waiting for transfers between devices: 33.5 us -> none  [the longest x1 18 us: shards(): lax.all_to_all(outbound, 'box', split_axis=3, concat_axis=0, tiled=True)]
    and x27 -> x0, other arithmetic: 18.8 us -> none  [add_term(): source = jnp.take(source_field, source_ids, axis=0)]
    another operation x4 -> x0, loops' own time: 13.3 us -> none  [the longest x1 12.3 us: shards(): matrices = lax.map(build_matrix, jnp.arange(block_count, dtype=jnp.int32))]
  transfers between devices with their start and end apart: 6 -> 4, of which waited for: 4 -> 3; matrix products, arithmetic and copies ran while one was open for 9% -> 2% of each run, Pallas kernels for 0% -> 0%
where the time goes in v1:
time: 89.5 us; the launch traced here: 89.2 us
  Pallas kernels  60.5 us (68%)
  starting transfers between devices  13.2 us (15%)
  local copies, waits for them, and re-layouts  7.83 us (9%)
  waiting for transfers between devices  6.9 us (8%)
    pallas_call x1, Pallas kernels, shards(): pl.pallas_call(exchange_kernel, out_shape=jax.ShapeDtypeStruct((chunks, p...  36 us
    pallas_call x1, Pallas kernels, shards(): pl.pallas_call(spread_kernel, out_shape=jax.ShapeDtypeStruct((rows, width...  13.7 us
    pallas_call x1, Pallas kernels, shards(): pl.pallas_call(aggregate_kernel, out_shape=jax.ShapeDtypeStruct((chunks,...  10.8 us
    ppermute x1, starting transfers between devices, shards(): low = lax.ppermute(by_box[:, strip_child - HW:], 'dir', forward)  6.21 us
    ppermute x1, starting transfers between devices, shards(): lax.ppermute(widened[:, strip_child + HW:strip_child + 2 * HW], 'dir', fo...  4.42 us
    ppermute x1, waiting for transfers between devices, shards(): from_above = lax.ppermute(widened[:, :HW], 'dir', backward)  4.13 us
    ppermute x1, waiting for transfers between devices, shards(): lax.ppermute(widened[:, strip_child + HW:strip_child + 2 * HW], 'dir', fo...  2.56 us
    transpose x1, local copies, waits for them, and re-layouts, shards(): by_box = jnp.transpose(child_field, (2, 0, 1, 3)).reshape(rows, strip_child)  2.03 us
  transfers between devices with their start and end apart: 4, of which 3 were waited for; matrix products, arithmetic and copies ran while one was open for 2% of the time, Pallas kernels for 0%

profile of v1, /device:TPU:0, one launch (start us, length us, event | category | flops | bytes accessed | tf_op | source)
XLA Modules:
  0.0 89.2 jit_solution(17619547910207135557)
XLA Ops:
  0.0 2.0 %copy.16 = f32[32,2,4,1152]{3,2,1,0:T(4,128)S(1)} copy(f32[32,2,4,1152]{3,0,2,1:T(8,128)} %bitcast.4) | data formatting | bytes 2359296 | tf_op jit(solution)/shard_map/transpose | solution.py:275
  2.0 0.0 copy-start.5
  2.1 0.4 reshape.7
  2.5 0.1 fusion.2
  2.6 1.3 %collective-permute-start.1 = (f32[256,8]{1,0:T(8,128)S(1)}, f32[256,8]{1,0:T(8,128)S(1)}, u32[]{:S(2)}, u32[]{:S(2)}) collective-permute-start(f32[256,8]{1,0:T(8,128)S(1)} %get-tuple-element.7), channel_id=1, source_target_pairs={{1,0},{2,1},{3,2},{5,4},{6,5},{7,6},{9,8},{10,9},{11,10},{13,12},{... | collective-permute-start | bytes 24584 | tf_op jit(solution)/shard_map/ppermute | solution.py:277
  3.9 6.2 %collective-permute-start = (f32[256,8]{1,0:T(8,128)S(1)}, f32[256,8]{1,0:T(8,128)}, u32[]{:S(2)}, u32[]{:S(2)}) collective-permute-start(f32[256,8]{1,0:T(8,128)S(1)} %get-tuple-element.8), channel_id=1, source_target_pairs={{0,1},{1,2},{2,3},{4,5},{5,6},{6,7},{8,9},{9,10},{10,11},{12,13},{... | collective-permute-start | bytes 24584 | tf_op jit(solution)/shard_map/ppermute | solution.py:276
  10.1 0.1 copy.17
  10.2 0.1 eq.15
  10.3 1.4 %fusion.3 = (f32[4,4608]{1,0:T(4,128)S(1)}, f32[4,4608]{1,0:T(4,128)S(1)}) fusion(f32[4,4608]{1,0:T(4,128)} %param.9), kind=kLoop, calls=%fused_computation.8 | loop fusion | bytes 221184 | tf_op jit(solution)/shard_map/sin | solution.py:281
  11.7 0.1 select_reduce_fusion.slot_ref
  11.8 0.2 copy.18.table_ref
  12.0 0.2 collective-permute-done
  12.2 1.8 %concatenate.3.x_ref = f32[256,1280]{1,0:T(8,128)S(1)} concatenate(f32[256,8]{1,0:T(8,128)} %collective-permute-done, f32[256,1152]{1,0:T(8,128)} %copy-done.3, f32[256,8]{1,0:T(8,128)S(1)} %collective-permute-done.1, f32[256,112]{1,0:T(8,128)S(1)} %broadcast_in_dim.17), dimensions={1} | concatenate | bytes 2621440 | tf_op jit(solution)/shard_map/concatenate | solution.py:278
  14.1 10.8 %shard_map.73.out_ref = f32[36,8,8,128]{3,2,1,0:T(8,128)S(1)} custom-call(f32[256,1280]{1,0:T(8,128)S(1)} %concatenate.3.x_ref, f32[4,4608]{1,0:T(4,128)S(1)} %get-tuple-element.10.cos_ref, f32[4,4608]{1,0:T(4,128)S(1)} %get-tuple-element.9.sin_ref, s32[6,4608]{1,0:T(8,128)S(1)} %copy-done, f32[6,4608]{1,0:T(8,128)S(1)} %copy-done.1, ...), custom_call_target="tpu_custom_call" | custom-call | tf_op jit(solution)/shard_map/pallas_call | solution.py:287
  24.9 36.0 %shard_map.74.in_ref = f32[36,8,8,128]{3,2,1,0:T(8,128)S(1)} custom-call(f32[36,8,8,128]{3,2,1,0:T(8,128)S(1)} %shard_map.73.out_ref, s32[27,64]{1,0:T(8,128)S(1)} %copy-done.2, f32[2,27,4608]{2,1,0:T(8,128)S(1)} %copy.18.table_ref), custom_call_target="tpu_custom_call" | custom-call | tf_op jit(solution)/shard_map/pallas_call | solution.py:301
  60.9 13.7 %shard_map.75 = f32[256,1280]{1,0:T(8,128)S(1)} custom-call(f32[36,8,8,128]{3,2,1,0:T(8,128)S(1)} %shard_map.74.in_ref, f32[4,4608]{1,0:T(4,128)S(1)} %get-tuple-element.10.cos_ref, f32[4,4608]{1,0:T(4,128)S(1)} %get-tuple-element.9.sin_ref, s32[6,4608]{1,0:T(8,128)S(1)} %copy-done, f32[6,4608]{1,0:T(8,128)S(1)} %copy-done.1, s32[32]{0:T(128)S(1)} %select_reduce_fusion.slot_ref), custom_call_target="tpu_custom_call" | custom-call | tf_op jit(solution)/shard_map/pallas_call | solution.py:320
  74.7 0.1 fusion.1
  74.8 4.4 %collective-permute-start.2 = (f32[256,8]{1,0:T(8,128)S(1)}, f32[256,8]{1,0:T(8,128)S(1)}, u32[]{:S(2)}, u32[]{:S(2)}) collective-permute-start(f32[256,8]{1,0:T(8,128)S(1)} %get-tuple-element.5), channel_id=1, source_target_pairs={{0,1},{1,2},{2,3},{4,5},{5,6},{6,7},{8,9},{9,10},{10,11},{12,13},{... | collective-permute-start | bytes 24584 | tf_op jit(solution)/shard_map/ppermute | solution.py:334
  79.2 1.3 %collective-permute-start.3 = (f32[256,8]{1,0:T(8,128)S(1)}, f32[256,8]{1,0:T(8,128)S(1)}, u32[]{:S(2)}, u32[]{:S(2)}) collective-permute-start(f32[256,8]{1,0:T(8,128)S(1)} %get-tuple-element.6), channel_id=1, source_target_pairs={{1,0},{2,1},{3,2},{5,4},{6,5},{7,6},{9,8},{10,9},{11,10},{13,12},{... | collective-permute-start | bytes 24584 | tf_op jit(solution)/shard_map/ppermute | solution.py:335
  80.5 2.6 %collective-permute-done.2 = f32[256,8]{1,0:T(8,128)S(1)} collective-permute-done((f32[256,8]{1,0:T(8,128)S(1)}, f32[256,8]{1,0:T(8,128)S(1)}, u32[]{:S(2)}, u32[]{:S(2)}) %collective-permute-start.2) | collective-permute-done | bytes 8224 | tf_op jit(solution)/shard_map/ppermute | solution.py:334
  83.1 4.1 %collective-permute-done.3 = f32[256,8]{1,0:T(8,128)S(1)} collective-permute-done((f32[256,8]{1,0:T(8,128)S(1)}, f32[256,8]{1,0:T(8,128)S(1)}, u32[]{:S(2)}, u32[]{:S(2)}) %collective-permute-start.3) | collective-permute-done | bytes 8224 | tf_op jit(solution)/shard_map/ppermute | solution.py:335
  87.2 0.4 fusion
  87.6 0.3 reshape.8
  87.9 1.2 %copy.21 = f32[32,2,4,1152]{3,0,2,1:T(8,128)} copy(f32[32,2,4,1152]{3,2,1,0:T(4,128)S(1)} %reshape.8) | data formatting | bytes 2359296 | tf_op jit(solution)/shard_map/reshape | solution.py:339
  (14 shorter events, 0.0 us)
Async XLA Ops:
  2.0 8.1 %copy-start.5 = (s32[8,4]{0,1:T(4,128)S(1)}, s32[8,4]{0,1:T(4,128)}, u32[]{:S(2)}) copy-start(s32[8,4]{0,1:T(4,128)} %param.8) | copy-start | bytes 388
  2.0 9.7 %copy-start.4 = (f32[2,27,4608]{2,0,1:T(2,128)S(1)}, f32[2,27,4608]{2,0,1:T(2,128)}, u32[]{:S(2)}) copy-start(f32[2,27,4608]{2,0,1:T(2,128)} %param.13) | copy-start | bytes 2985988
  2.5 7.7 %copy-start.3 = (f32[256,1152]{1,0:T(8,128)}, f32[256,1152]{1,0:T(8,128)S(1)}, u32[]{:S(2)}) copy-start(f32[256,1152]{1,0:T(8,128)S(1)} %reshape.7) | copy-start | bytes 3538948
  2.6 9.4 %collective-permute-start.1 = (f32[256,8]{1,0:T(8,128)S(1)}, f32[256,8]{1,0:T(8,128)S(1)}, u32[]{:S(2)}, u32[]{:S(2)}) collective-permute-start(f32[256,8]{1,0:T(8,128)S(1)} %get-tuple-element.7), channel_id=1, source_target_pairs={{1,0},{2,1},{3,2},{5,4},{6,5},{7,6},{9,8},{10,9},{11,10},{13,12},{... | collective-permute-start | bytes 24584 | tf_op jit(solution)/shard_map/ppermute | solution.py:277
  3.9 8.3 %collective-permute-start = (f32[256,8]{1,0:T(8,128)S(1)}, f32[256,8]{1,0:T(8,128)}, u32[]{:S(2)}, u32[]{:S(2)}) collective-permute-start(f32[256,8]{1,0:T(8,128)S(1)} %get-tuple-element.8), channel_id=1, source_target_pairs={{0,1},{1,2},{2,3},{4,5},{5,6},{6,7},{8,9},{9,10},{10,11},{12,13},{... | collective-permute-start | bytes 24584 | tf_op jit(solution)/shard_map/ppermute | solution.py:276
  12.2 1.9 %copy-start = (s32[6,4608]{1,0:T(8,128)S(1)}, s32[6,4608]{1,0:T(8,128)}, u32[]{:S(2)}) copy-start(s32[6,4608]{1,0:T(8,128)} %index_ref.3) | copy-start | bytes 331780
  12.2 1.9 %copy-start.1 = (f32[6,4608]{1,0:T(8,128)S(1)}, f32[6,4608]{1,0:T(8,128)}, u32[]{:S(2)}) copy-start(f32[6,4608]{1,0:T(8,128)} %weight_ref.3) | copy-start | bytes 331780
  14.1 10.8 %copy-start.2 = (s32[27,64]{1,0:T(8,128)S(1)}, s32[27,64]{1,0:T(8,128)}, u32[]{:S(2)}) copy-start(s32[27,64]{1,0:T(8,128)} %list_ref.1) | copy-start | bytes 20740
  74.8 8.3 %collective-permute-start.2 = (f32[256,8]{1,0:T(8,128)S(1)}, f32[256,8]{1,0:T(8,128)S(1)}, u32[]{:S(2)}, u32[]{:S(2)}) collective-permute-start(f32[256,8]{1,0:T(8,128)S(1)} %get-tuple-element.5), channel_id=1, source_target_pairs={{0,1},{1,2},{2,3},{4,5},{5,6},{6,7},{8,9},{9,10},{10,11},{12,13},{... | collective-permute-start | bytes 24584 | tf_op jit(solution)/shard_map/ppermute | solution.py:334
  79.2 8.0 %collective-permute-start.3 = (f32[256,8]{1,0:T(8,128)S(1)}, f32[256,8]{1,0:T(8,128)S(1)}, u32[]{:S(2)}, u32[]{:S(2)}) collective-permute-start(f32[256,8]{1,0:T(8,128)S(1)} %get-tuple-element.6), channel_id=1, source_target_pairs={{1,0},{2,1},{3,2},{5,4},{6,5},{7,6},{9,8},{10,9},{11,10},{13,12},{... | collective-permute-start | bytes 24584 | tf_op jit(solution)/shard_map/ppermute | solution.py:335

commit v2 on v1

v2 whole, which is shorter than its diff:
```python
import jax
import jax.numpy as jnp
from jax import lax
from jax.experimental import pallas as pl
from jax.experimental.pallas import tpu as pltpu
from jax.sharding import PartitionSpec as P

HW = 8
LANES = 128
RATIO = 4
BAND = LANES // RATIO + 2 * HW
WINDOW = 2 * LANES
VMEM = pl.BlockSpec(memory_space=pltpu.VMEM)
SMEM = pl.BlockSpec(memory_space=pltpu.SMEM)


def rotated(value):
    half = value.shape[0] // 2
    sign = jnp.where(lax.broadcasted_iota(jnp.int32, value.shape, 0) < half, -1.0, 1.0)
    return pltpu.roll(value, half, 0) * sign


def split(value):
    high = value.astype(jnp.bfloat16)
    low = (value - high.astype(jnp.float32)).astype(jnp.bfloat16)
    return high, low


def lanes_of(chunk):
    return pl.ds(pl.multiple_of(chunk * LANES, LANES), LANES)


def band_of(chunk, first_child, index_ref, weight_ref):
    place = lax.broadcasted_iota(jnp.int32, (BAND, LANES), 0)
    base = first_child + chunk * (LANES // RATIO) - HW
    band = jnp.zeros((BAND, LANES), jnp.float32)
    for stencil_at in range(index_ref.shape[0]):
        row = index_ref[stencil_at : stencil_at + 1, lanes_of(chunk)] - base
        weight = weight_ref[stencil_at : stencil_at + 1, lanes_of(chunk)]
        band = band + jnp.where(row == place, weight, 0.0)
    return band


def band_rows(corner):
    return pl.ds(pl.multiple_of(corner * (LANES // RATIO), LANES // RATIO), BAND)


def whole_kernel(
    x_ref, cos_ref, sin_ref, index_ref, weight_ref, table_ref, kids_ref, parent_ref, kid_ref,
    list_ref, result_ref,
    high_ref, low_ref, bands, matrix_ref, field_ref, outgoing, answer, operator, back, piece, phase,
    values_ref, wide_ref, edge_in, edge_out, edge_back,
    sent, arrived, returned, home, near, edge_sent, edge_arrived, *source
):
    chunks, parents = outgoing.shape[:2]
    strip = x_ref.shape[1]
    rows = x_ref.shape[0]
    boxes = parent_ref.shape[0]
    parts = rows // boxes
    kids = cos_ref.shape[0]
    terms = list_ref.shape[0]
    rounds = len(source)
    count = lax.axis_size("box")
    me = lax.axis_index("box")
    layers = lax.axis_size("dir")
    layer = lax.axis_index("dir")
    first_child = layer * strip
    mesh_id = pl.DeviceIdType.MESH
    has_below = layer > 0
    has_above = layer < layers - 1

    def first(owner):
        return chunks * owner // count

    def held(owner):
        return first(owner + 1) - first(owner)

    def chunk_of(owner, at):
        return first(owner) + jnp.where(owner < count // 2, held(owner) - 1 - at, at)

    def other(step):
        return lax.rem(me + step, count)

    def block(owner):
        return pl.ds(owner * parents, parents)

    def each(act, stop=count):
        def step_of(step, carry):
            act(other(step))
            return carry

        lax.fori_loop(1, stop, step_of, 0)

    barrier = pltpu.get_barrier_semaphore()
    each(lambda owner: pl.semaphore_signal(
        barrier, inc=1, device_id={"box": owner}, device_id_type=mesh_id))

    @pl.when(has_below)
    def _():
        pl.semaphore_signal(barrier, inc=1, device_id={"dir": layer - 1}, device_id_type=mesh_id)

    @pl.when(has_above)
    def _():
        pl.semaphore_signal(barrier, inc=1, device_id={"dir": layer + 1}, device_id_type=mesh_id)

    neighbours = jnp.where(has_below, 1, 0) + jnp.where(has_above, 1, 0)
    pl.semaphore_wait(barrier, count - 1 + neighbours)

    def to_above(at, src, dst):
        return pltpu.make_async_remote_copy(
            src_ref=src, dst_ref=dst.at[0], send_sem=edge_sent.at[at, 0],
            recv_sem=edge_arrived.at[at, 0], device_id={"dir": layer + 1}, device_id_type=mesh_id)

    def to_below(at, src, dst):
        return pltpu.make_async_remote_copy(
            src_ref=src, dst_ref=dst.at[1], send_sem=edge_sent.at[at, 1],
            recv_sem=edge_arrived.at[at, 1], device_id={"dir": layer - 1}, device_id_type=mesh_id)

    top = x_ref.at[:, strip - LANES :]
    bottom = x_ref.at[:, :LANES]
    pl.when(has_above)(lambda: to_above(0, top, edge_in).start())
    pl.when(has_below)(lambda: to_below(0, bottom, edge_in).start())

    def outbound(owner, at):
        chunk = chunk_of(owner, at)
        return pltpu.make_async_remote_copy(
            src_ref=outgoing.at[chunk], dst_ref=source[at].at[block(me)],
            send_sem=sent.at[chunk], recv_sem=arrived.at[at, me],
            device_id={"box": owner}, device_id_type=mesh_id)

    def inbound(owner, at):
        chunk = chunk_of(me, at)
        return pltpu.make_async_remote_copy(
            src_ref=outgoing.at[chunk], dst_ref=source[at].at[block(owner)],
            send_sem=sent.at[chunk], recv_sem=arrived.at[at, owner],
            device_id={"box": owner}, device_id_type=mesh_id)

    def homebound(owner, at):
        chunk = chunk_of(me, at)
        return pltpu.make_async_remote_copy(
            src_ref=answer.at[at, block(owner)], dst_ref=back.at[chunk],
            send_sem=returned.at[at, owner], recv_sem=home.at[chunk],
            device_id={"box": owner}, device_id_type=mesh_id)

    def from_owner(owner, at):
        chunk = chunk_of(owner, at)
        return pltpu.make_async_remote_copy(
            src_ref=answer.at[at, block(me)], dst_ref=back.at[chunk],
            send_sem=returned.at[at, me], recv_sem=home.at[chunk],
            device_id={"box": owner}, device_id_type=mesh_id)

    def own_out(at):
        return pltpu.make_async_copy(outgoing.at[chunk_of(me, at)], source[at].at[block(me)],
                                     near.at[at])

    def own_back(at):
        return pltpu.make_async_copy(answer.at[at, block(me)], back.at[chunk_of(me, at)],
                                     near.at[at])

    extended = jnp.concatenate([x_ref[...], jnp.zeros((rows, LANES), jnp.float32)], axis=1)
    high, low = split(pltpu.roll(extended, HW, 1))
    high_ref[...] = high
    low_ref[...] = low
    matrix_ref[...] = jnp.zeros_like(matrix_ref)
    wide_ref[...] = jnp.zeros_like(wide_ref)
    lane = lax.broadcasted_iota(jnp.int32, (rows, LANES), 1)

    def put_edge(side, columns, begin):
        new_high, new_low = split(pltpu.roll(edge_in[side], HW, 1))
        chosen = ((lane >= begin) & (lane < begin + HW)).astype(jnp.bfloat16)
        keep = 1 - chosen
        high_ref[:, columns] = high_ref[:, columns] * keep + new_high * chosen
        low_ref[:, columns] = low_ref[:, columns] * keep + new_low * chosen

    def window_of(chunk):
        return pl.ds(pl.multiple_of(chunk // RATIO * LANES, LANES), WINDOW)

    def aggregate(chunk):
        corner = lax.rem(chunk, RATIO)
        columns = window_of(chunk)
        band_high, band_low = split(band_of(chunk, first_child, index_ref, weight_ref))
        bands[chunk, :, :LANES] = band_high
        bands[chunk, :, LANES:] = band_low
        matrix_ref[corner, band_rows(corner), :LANES] = band_high
        matrix_ref[corner, band_rows(corner), LANES:] = band_low
        both = jnp.dot(high_ref[:, columns], matrix_ref[corner],
                       preferred_element_type=jnp.float32)
        rest = jnp.dot(low_ref[:, columns], matrix_ref[corner, :, :LANES],
                       preferred_element_type=jnp.float32)
        field_ref[...] = (both[:, :LANES] + (both[:, LANES:] + rest)).reshape(field_ref.shape)
        cosines = cos_ref[:, lanes_of(chunk)]
        sines = sin_ref[:, lanes_of(chunk)]
        for parent in range(parents):
            straight = turned = 0.0
            for kid in range(kids):
                value = field_ref[kids_ref[parent, kid]]
                straight = straight + cosines[kid : kid + 1] * value
                turned = turned + sines[kid : kid + 1] * value
            outgoing[chunk, parent] = straight + rotated(turned)

    for at in range(rounds):
        if at == max(0, rounds - 2):

            @pl.when(has_below)
            def _():
                to_above(0, top, edge_in).wait_recv()
                put_edge(0, pl.ds(0, LANES), 0)

            @pl.when(has_above)
            def _():
                to_below(0, bottom, edge_in).wait_recv()
                put_edge(1, pl.ds(strip, LANES), HW)

        def produce(owner):
            @pl.when(at < held(owner))
            def _():
                aggregate(chunk_of(owner, at))
                pl.when(owner != me)(lambda: outbound(owner, at).start())
                pl.when(owner == me)(lambda: own_out(at).start())

        each(produce, count + 1)

    def translate_group(at, owner):
        unroll = 3 if terms % 3 == 0 else 1

        def some(term_at, carry):
            straight, turned = list(carry[0]), list(carry[1])
            for part in range(unroll):
                term = term_at * unroll + part
                op_real = operator[0, term]
                op_imag = operator[1, term]
                for parent in range(parents):
                    value = source[at][list_ref[term, owner * parents + parent]]
                    straight[parent] = straight[parent] + op_real * value
                    turned[parent] = turned[parent] + op_imag * value
            return tuple(straight), tuple(turned)

        zero = jnp.zeros(answer.shape[2:], jnp.float32)
        straight, turned = lax.fori_loop(
            0, terms // unroll, some, ((zero,) * parents, (zero,) * parents))
        for parent in range(parents):
            answer[at, owner * parents + parent] = straight[parent] + rotated(turned[parent])

    for at in range(rounds):

        @pl.when(at < held(me))
        def _():
            each(lambda owner: inbound(owner, at).wait_recv())
            own_out(at).wait()
            for half in range(2):
                for term in range(terms):
                    operator[half, term] = jnp.broadcast_to(
                        table_ref[half, term : term + 1, lanes_of(chunk_of(me, at))],
                        operator.shape[2:])

            def reply(owner):
                translate_group(at, owner)
                pl.when(owner != me)(lambda: homebound(owner, at).start())
                pl.when(owner == me)(lambda: own_back(at).start())

            each(reply, count + 1)

    def spread(chunk):
        corner = lax.rem(chunk, RATIO)
        matrix_ref[corner, band_rows(corner), :] = bands[chunk]
        for parent in range(parents):
            value = back[chunk, parent]
            piece[0, parent] = value
            piece[1, parent] = rotated(value)
        for kid in range(kids):
            for half, angles in enumerate((cos_ref, sin_ref)):
                phase[half, kid] = jnp.broadcast_to(
                    angles[kid : kid + 1, lanes_of(chunk)], phase.shape[2:])
        for box in range(boxes):
            parent, kid = parent_ref[box], kid_ref[box]
            values_ref[box * parts : (box + 1) * parts, :] = (
                phase[0, kid] * piece[0, parent] - phase[1, kid] * piece[1, parent])
        high, low = split(values_ref[...])
        dims = (((1,), (1,)), ((), ()))
        product = lax.dot_general(jnp.concatenate([high, high], axis=1), matrix_ref[corner], dims,
                                  preferred_element_type=jnp.float32)
        product = product + lax.dot_general(low, matrix_ref[corner, :, :LANES], dims,
                                            preferred_element_type=jnp.float32)
        wide_ref[:, window_of(chunk)] += product

    above_part = edge_out.at[0]
    below_part = edge_out.at[1]
    order = sorted(range(rounds), key=lambda at: (at > 0, at < rounds - 2, at))
    for place, at in enumerate(order):

        def finish(owner):
            @pl.when(at < held(owner))
            def _():
                @pl.when(owner != me)
                def _():
                    outbound(owner, at).wait_send()
                    from_owner(owner, at).wait_recv()

                pl.when(owner == me)(lambda: own_back(at).wait())
                spread(chunk_of(owner, at))

        each(finish, count + 1)

        @pl.when(at < held(me))
        def _():
            each(lambda owner: homebound(owner, at).wait_send())

        if place == min(2, rounds - 1):

            @pl.when(has_above)
            def _():
                edge_out[0] = wide_ref[:, strip:]
                to_above(1, above_part, edge_back).start()

            @pl.when(has_below)
            def _():
                edge_out[1] = wide_ref[:, :LANES]
                to_below(1, below_part, edge_back).start()

    @pl.when(has_below)
    def _():
        to_above(1, above_part, edge_back).wait_recv()
        mine = (lane >= HW) & (lane < 2 * HW)
        wide_ref[:, :LANES] += jnp.where(mine, edge_back[0], 0.0)
        to_below(0, bottom, edge_in).wait_send()
        to_below(1, below_part, edge_back).wait_send()

    @pl.when(has_above)
    def _():
        to_below(1, below_part, edge_back).wait_recv()
        wide_ref[:, strip:] += jnp.where(lane < HW, edge_back[1], 0.0)
        to_above(0, top, edge_in).wait_send()
        to_above(1, above_part, edge_back).wait_send()

    result_ref[...] = pltpu.roll(wide_ref[...], strip + LANES - HW, 1)[:, :strip]


def shards(
    child_field, child_of, shift_angle, interp_index, interp_weight, interaction_list, translation
):
    box_count = lax.axis_size("box")
    box_index = lax.axis_index("box")
    halves, fields, own_boxes, strip_child = child_field.shape
    parents, kids = child_of.shape
    chunks = interp_index.shape[1] // LANES
    parts = halves * fields
    rows = own_boxes * parts
    rounds = -(-chunks // box_count)
    width = strip_child + LANES
    terms = interaction_list.shape[0]
    f32, bf16 = jnp.float32, jnp.bfloat16

    by_box = jnp.transpose(child_field, (2, 0, 1, 3)).reshape(rows, strip_child)
    local = child_of - box_index * own_boxes
    slots = jnp.sum(
        jnp.where(local.reshape(-1)[:, None] == lax.iota(jnp.int32, own_boxes)[None, :],
                  lax.iota(jnp.int32, parents * kids)[:, None], 0), axis=0).astype(jnp.int32)

    result = pl.pallas_call(
        whole_kernel,
        out_shape=jax.ShapeDtypeStruct((rows, strip_child), f32),
        in_specs=[VMEM] * 6 + [SMEM] * 4,
        out_specs=VMEM,
        scratch_shapes=[
            pltpu.VMEM((rows, width), bf16),
            pltpu.VMEM((rows, width), bf16),
            pltpu.VMEM((chunks, BAND, 2 * LANES), bf16),
            pltpu.VMEM((RATIO, WINDOW, 2 * LANES), bf16),
            pltpu.VMEM((own_boxes, parts, LANES), f32),
            pltpu.VMEM((chunks, parents, parts, LANES), f32),
            pltpu.VMEM((rounds, box_count * parents, parts, LANES), f32),
            pltpu.VMEM((2, terms, parts, LANES), f32),
            pltpu.VMEM((chunks, parents, parts, LANES), f32),
            pltpu.VMEM((2, parents, parts, LANES), f32),
            pltpu.VMEM((2, kids, parts, LANES), f32),
            pltpu.VMEM((rows, LANES), f32),
            pltpu.VMEM((rows, width), f32),
            pltpu.VMEM((2, rows, LANES), f32),
            pltpu.VMEM((2, rows, LANES), f32),
            pltpu.VMEM((2, rows, LANES), f32),
            pltpu.SemaphoreType.DMA((chunks,)),
            pltpu.SemaphoreType.DMA((rounds, box_count)),
            pltpu.SemaphoreType.DMA((rounds, box_count)),
            pltpu.SemaphoreType.DMA((chunks,)),
            pltpu.SemaphoreType.DMA((rounds,)),
            pltpu.SemaphoreType.DMA((2, 2)),
            pltpu.SemaphoreType.DMA((2, 2)),
            *[pltpu.VMEM((box_count * parents, parts, LANES), f32)] * rounds,
        ],
        compiler_params=pltpu.CompilerParams(
            collective_id=0, has_side_effects=True, vmem_limit_bytes=48 * 1024 * 1024),
    )(by_box, jnp.cos(shift_angle), jnp.sin(shift_angle), interp_index, interp_weight, translation,
      local, slots // kids, slots % kids, interaction_list)
    return jnp.transpose(result.reshape(own_boxes, halves, fields, strip_child), (1, 2, 0, 3))


def solution(mesh):
    in_specs = (
        P(None, None, "box", "dir"),
        P("box", None),
        P(None, "dir"),
        P(None, "dir"),
        P(None, "dir"),
        P(),
        P(None, None, "dir"),
    )
    out_specs = P(None, None, "box", "dir")
    return jax.shard_map(shards, mesh=mesh, in_specs=in_specs, out_specs=out_specs, check_vma=False)
```

time: 89.5 us -> 64 us (0.72)
  the two profiles are of different devices: /device:TPU:0 before, /device:TPU:1 now
where the time goes in v2:
time: 64 us; the launch traced here: 63.8 us
  Pallas kernels  55.6 us (87%)
  local copies, waits for them, and re-layouts  8.02 us (13%)
    pallas_call x1, Pallas kernels, shards(): pl.pallas_call(whole_kernel, out_shape=jax.ShapeDtypeStruct((rows, strip_...  55.6 us
    unnamed x10, local copies, waits for them, and re-layouts  2.52 us
    transpose x1, local copies, waits for them, and re-layouts, shards(): by_box = jnp.transpose(child_field, (2, 0, 1, 3)).reshape(rows, strip_child)  2.03 us
    reshape x2, local copies, waits for them, and re-layouts, shards(): result.reshape(own_boxes, halves, fields, strip_child)  1.57 us
    sin x1, local copies, waits for them, and re-layouts, shards(): jnp.sin(shift_angle)  1.4 us

profile of v2, /device:TPU:1, one launch (start us, length us, event | category | flops | bytes accessed | tf_op | source)
XLA Modules:
  0.0 63.8 jit_solution(4999422125433095499)
XLA Ops:
  0.0 0.8 %copy.17 = s32[8,4]{1,0:T(8,128)S(1)} copy(s32[8,4]{0,1:T(4,128)} %param.8) | data formatting | bytes 256 | tf_op args[1]
  0.8 0.1 eq.17
  0.8 0.1 select_reduce_fusion
  1.0 1.4 %fusion = (f32[4,4608]{1,0:T(4,128)S(1)}, f32[4,4608]{1,0:T(4,128)S(1)}) fusion(f32[4,4608]{1,0:T(4,128)} %param.9), kind=kLoop, calls=%fused_computation.9 | loop fusion | bytes 221184 | tf_op jit(solution)/shard_map/sin | solution.py:392
  2.4 2.0 %copy.16 = f32[32,2,4,1152]{3,2,1,0:T(4,128)S(1)} copy(f32[32,2,4,1152]{3,0,2,1:T(8,128)} %bitcast.4) | data formatting | bytes 2359296 | tf_op jit(solution)/shard_map/transpose | solution.py:353
  4.4 0.0 copy-start.3
  4.4 0.4 reshape.7.x_ref
  4.8 0.8 %copy-done.3 = f32[2,27,4608]{2,0,1:T(2,128)S(1)} copy-done((f32[2,27,4608]{2,0,1:T(2,128)S(1)}, f32[2,27,4608]{2,0,1:T(2,128)}, u32[]{:S(2)}) %copy-start.3) | copy-done | bytes 995352
  5.6 0.0 copy-start
  5.6 0.0 copy-start.1
  5.6 0.0 copy-start.2
  5.6 0.2 copy.18.table_ref
  5.8 0.7 %copy-done = s32[6,4608]{1,0:T(8,128)S(1)} copy-done((s32[6,4608]{1,0:T(8,128)S(1)}, s32[6,4608]{1,0:T(8,128)}, u32[]{:S(2)}) %copy-start) | copy-done | bytes 110616
  6.5 0.1 copy-done.1
  6.6 0.0 copy-done.2
  6.6 55.6 %shard_map.73 = f32[256,1152]{1,0:T(8,128)S(1)} custom-call(f32[256,1152]{1,0:T(8,128)S(1)} %reshape.7.x_ref, f32[4,4608]{1,0:T(4,128)S(1)} %get-tuple-element.6.cos_ref, f32[4,4608]{1,0:T(4,128)S(1)} %get-tuple-element.5.sin_ref, s32[6,4608]{1,0:T(8,128)S(1)} %copy-done, f32[6,4608]{1,0:T(8,128)S(1)} %copy-done.1, f32[2,27,4608]{2,1,0:T(8,128)S(1)} %copy.18.table_ref, ...), custom_call_target="tpu_custom_call" | custom-call | tf_op jit(solution)/shard_map/pallas_call | solution.py:359
  62.2 0.3 reshape.8
  62.6 1.2 %copy.21 = f32[32,2,4,1152]{3,0,2,1:T(8,128)} copy(f32[32,2,4,1152]{3,2,1,0:T(4,128)S(1)} %reshape.8) | data formatting | bytes 2359296 | tf_op jit(solution)/shard_map/reshape | solution.py:394
  (2 shorter events, 0.0 us)
Async XLA Ops:
  4.4 1.2 %copy-start.3 = (f32[2,27,4608]{2,0,1:T(2,128)S(1)}, f32[2,27,4608]{2,0,1:T(2,128)}, u32[]{:S(2)}) copy-start(f32[2,27,4608]{2,0,1:T(2,128)} %param.13) | copy-start | bytes 2985988
  5.6 0.9 %copy-start = (s32[6,4608]{1,0:T(8,128)S(1)}, s32[6,4608]{1,0:T(8,128)}, u32[]{:S(2)}) copy-start(s32[6,4608]{1,0:T(8,128)} %index_ref.1) | copy-start | bytes 331780
  5.6 1.0 %copy-start.1 = (f32[6,4608]{1,0:T(8,128)S(1)}, f32[6,4608]{1,0:T(8,128)}, u32[]{:S(2)}) copy-start(f32[6,4608]{1,0:T(8,128)} %weight_ref.1) | copy-start | bytes 331780
  5.6 1.0 %copy-start.2 = (s32[27,64]{1,0:T(8,128)S(1)}, s32[27,64]{1,0:T(8,128)}, u32[]{:S(2)}) copy-start(s32[27,64]{1,0:T(8,128)} %list_ref.1) | copy-start | bytes 20740

commit v3 on v2

--- a/solution.py
+++ b/solution.py
@@ -48,8 +48,8 @@
 def whole_kernel(
     x_ref, cos_ref, sin_ref, index_ref, weight_ref, table_ref, kids_ref, parent_ref, kid_ref,
     list_ref, result_ref,
-    high_ref, low_ref, bands, matrix_ref, field_ref, outgoing, answer, operator, back, piece, phase,
-    values_ref, wide_ref, edge_in, edge_out, edge_back,
+    high_ref, low_ref, bands, matrix_0, matrix_1, field_0, field_1, outgoing, answer, operator, back,
+    piece_0, piece_1, phase_0, phase_1, values_0, values_1, wide_ref, edge_in, edge_out, edge_back,
     sent, arrived, returned, home, near, edge_sent, edge_arrived, *source
 ):
     chunks, parents = outgoing.shape[:2]
@@ -58,9 +58,15 @@
     boxes = parent_ref.shape[0]
     parts = rows // boxes
     kids = cos_ref.shape[0]
-    terms = list_ref.shape[0]
-    rounds = len(source)
+    terms = table_ref.shape[1]
+    rounds = answer.shape[0]
     count = lax.axis_size("box")
+    groups = [range(at, min(at + 2, rounds - 1)) for at in range(0, rounds - 1, 2)]
+    groups.append(range(rounds - 1, rounds))
+    slot_of = {at: (g, at - group[0]) for g, group in enumerate(groups) for at in group}
+    sets = [(matrix_0, field_0, piece_0, phase_0, values_0),
+            (matrix_1, field_1, piece_1, phase_1, values_1)]
+    many = 2 if count % 2 == 0 else 1
     me = lax.axis_index("box")
     layers = lax.axis_size("dir")
     layer = lax.axis_index("dir")
@@ -84,6 +90,17 @@
     def block(owner):
         return pl.ds(owner * parents, parents)
 
+    def landing(at, owner):
+        group, inner = slot_of[at]
+        return source[group].at[block(owner), inner]
+
+    def each_set(act):
+        def steps_of(step, carry):
+            act([other(step * many + 1 + k) for k in range(many)])
+            return carry
+
+        lax.fori_loop(0, count // many, steps_of, 0)
+
     def each(act, stop=count):
         def step_of(step, carry):
             act(other(step))
@@ -124,14 +141,14 @@
     def outbound(owner, at):
         chunk = chunk_of(owner, at)
         return pltpu.make_async_remote_copy(
-            src_ref=outgoing.at[chunk], dst_ref=source[at].at[block(me)],
+            src_ref=outgoing.at[chunk], dst_ref=landing(at, me),
             send_sem=sent.at[chunk], recv_sem=arrived.at[at, me],
             device_id={"box": owner}, device_id_type=mesh_id)
 
     def inbound(owner, at):
         chunk = chunk_of(me, at)
         return pltpu.make_async_remote_copy(
-            src_ref=outgoing.at[chunk], dst_ref=source[at].at[block(owner)],
+            src_ref=outgoing.at[chunk], dst_ref=landing(at, owner),
             send_sem=sent.at[chunk], recv_sem=arrived.at[at, owner],
             device_id={"box": owner}, device_id_type=mesh_id)
 
@@ -150,7 +167,7 @@
             device_id={"box": owner}, device_id_type=mesh_id)
 
     def own_out(at):
-        return pltpu.make_async_copy(outgoing.at[chunk_of(me, at)], source[at].at[block(me)],
+        return pltpu.make_async_copy(outgoing.at[chunk_of(me, at)], landing(at, me),
                                      near.at[at])
 
     def own_back(at):
@@ -161,7 +178,8 @@
     high, low = split(pltpu.roll(extended, HW, 1))
     high_ref[...] = high
     low_ref[...] = low
-    matrix_ref[...] = jnp.zeros_like(matrix_ref)
+    matrix_0[...] = jnp.zeros_like(matrix_0)
+    matrix_1[...] = jnp.zeros_like(matrix_1)
     wide_ref[...] = jnp.zeros_like(wide_ref)
     lane = lax.broadcasted_iota(jnp.int32, (rows, LANES), 1)
 
@@ -175,7 +193,8 @@
     def window_of(chunk):
         return pl.ds(pl.multiple_of(chunk // RATIO * LANES, LANES), WINDOW)
 
-    def aggregate(chunk):
+    def aggregate(chunk, scratch):
+        matrix_ref, field_ref = scratch[:2]
         corner = lax.rem(chunk, RATIO)
         columns = window_of(chunk)
         band_high, band_low = split(band_of(chunk, first_child, index_ref, weight_ref))
@@ -211,56 +230,71 @@
                 to_below(0, bottom, edge_in).wait_recv()
                 put_edge(1, pl.ds(strip, LANES), HW)
 
+        def ship(owner):
+            pl.when(owner != me)(lambda: outbound(owner, at).start())
+            pl.when(owner == me)(lambda: own_out(at).start())
+
         def produce(owner):
             @pl.when(at < held(owner))
             def _():
-                aggregate(chunk_of(owner, at))
-                pl.when(owner != me)(lambda: outbound(owner, at).start())
-                pl.when(owner == me)(lambda: own_out(at).start())
-
-        each(produce, count + 1)
-
-    def translate_group(at, owner):
-        unroll = 3 if terms % 3 == 0 else 1
-
-        def some(term_at, carry):
-            straight, turned = list(carry[0]), list(carry[1])
-            for part in range(unroll):
-                term = term_at * unroll + part
-                op_real = operator[0, term]
-                op_imag = operator[1, term]
-                for parent in range(parents):
-                    value = source[at][list_ref[term, owner * parents + parent]]
-                    straight[parent] = straight[parent] + op_real * value
-                    turned[parent] = turned[parent] + op_imag * value
-            return tuple(straight), tuple(turned)
-
-        zero = jnp.zeros(answer.shape[2:], jnp.float32)
-        straight, turned = lax.fori_loop(
-            0, terms // unroll, some, ((zero,) * parents, (zero,) * parents))
-        for parent in range(parents):
-            answer[at, owner * parents + parent] = straight[parent] + rotated(turned[parent])
-
-    for at in range(rounds):
-
-        @pl.when(at < held(me))
-        def _():
-            each(lambda owner: inbound(owner, at).wait_recv())
-            own_out(at).wait()
-            for half in range(2):
-                for term in range(terms):
-                    operator[half, term] = jnp.broadcast_to(
-                        table_ref[half, term : term + 1, lanes_of(chunk_of(me, at))],
-                        operator.shape[2:])
+                aggregate(chunk_of(owner, at), sets[0])
+                ship(owner)
+
+        def produce_set(owners):
+            for owner, scratch in zip(owners, sets):
+                aggregate(chunk_of(owner, at), scratch)
+            for owner in owners:
+                ship(owner)
+
+        if at < rounds - 1:
+            each_set(produce_set)
+        else:
+            each(produce, count + 1)
+
+    def translate_group(group, owner):
+        landed = source[group]
+        inner = range(len(groups[group]))
+        straight = {}
+        turned = {}
+        for term in range(terms):
+            op_real = [operator[at, 0, term] for at in inner]
+            op_imag = [operator[at, 1, term] for at in inner]
+            for parent in range(parents):
+                index = list_ref[(owner * terms + term) * parents + parent]
+                for at in inner:
+                    value = landed[index, at]
+                    real, imag = op_real[at] * value, op_imag[at] * value
+                    key = (parent, at)
+                    straight[key] = straight[key] + real if term else real
+                    turned[key] = turned[key] + imag if term else imag
+        for parent, at in straight:
+            answer[groups[group][at], owner * parents + parent] = (
+                straight[parent, at] + rotated(turned[parent, at]))
+
+    for group, members in enumerate(groups):
+
+        def serve():
+            for inner, at in enumerate(members):
+                each(lambda owner: inbound(owner, at).wait_recv())
+                own_out(at).wait()
+                for half in range(2):
+                    for term in range(terms):
+                        operator[inner, half, term] = jnp.broadcast_to(
+                            table_ref[half, term : term + 1, lanes_of(chunk_of(me, at))],
+                            operator.shape[3:])
 
             def reply(owner):
-                translate_group(at, owner)
-                pl.when(owner != me)(lambda: homebound(owner, at).start())
-                pl.when(owner == me)(lambda: own_back(at).start())
+                translate_group(group, owner)
+                for at in members:
+                    pl.when(owner != me)(lambda: homebound(owner, at).start())
+                    pl.when(owner == me)(lambda: own_back(at).start())
 
             each(reply, count + 1)
 
-    def spread(chunk):
+        pl.when(members[0] < held(me))(serve)
+
+    def spread(chunk, scratch):
+        matrix_ref, _, piece, phase, values_ref = scratch
         corner = lax.rem(chunk, RATIO)
         matrix_ref[corner, band_rows(corner), :] = bands[chunk]
         for parent in range(parents):
@@ -281,25 +315,40 @@
                                   preferred_element_type=jnp.float32)
         product = product + lax.dot_general(low, matrix_ref[corner, :, :LANES], dims,
                                             preferred_element_type=jnp.float32)
-        wide_ref[:, window_of(chunk)] += product
+        return product
 
     above_part = edge_out.at[0]
     below_part = edge_out.at[1]
     order = sorted(range(rounds), key=lambda at: (at > 0, at < rounds - 2, at))
     for place, at in enumerate(order):
 
+        def await_back(owner):
+            @pl.when(owner != me)
+            def _():
+                outbound(owner, at).wait_send()
+                from_owner(owner, at).wait_recv()
+
+            pl.when(owner == me)(lambda: own_back(at).wait())
+
         def finish(owner):
             @pl.when(at < held(owner))
             def _():
-                @pl.when(owner != me)
-                def _():
-                    outbound(owner, at).wait_send()
-                    from_owner(owner, at).wait_recv()
-
-                pl.when(owner == me)(lambda: own_back(at).wait())
-                spread(chunk_of(owner, at))
-
-        each(finish, count + 1)
+                await_back(owner)
+                chunk = chunk_of(owner, at)
+                wide_ref[:, window_of(chunk)] += spread(chunk, sets[0])
+
+        def finish_set(owners):
+            for owner in owners:
+                await_back(owner)
+            at_chunks = [chunk_of(owner, at) for owner in owners]
+            products = [spread(chunk, scratch) for chunk, scratch in zip(at_chunks, sets)]
+            for chunk, product in zip(at_chunks, products):
+                wide_ref[:, window_of(chunk)] += product
+
+        if at < rounds - 1:
+            each_set(finish_set)
+        else:
+            each(finish, count + 1)
 
         @pl.when(at < held(me))
         def _():
@@ -356,6 +405,8 @@
         jnp.where(local.reshape(-1)[:, None] == lax.iota(jnp.int32, own_boxes)[None, :],
                   lax.iota(jnp.int32, parents * kids)[:, None], 0), axis=0).astype(jnp.int32)
 
+    lists = jnp.transpose(interaction_list.reshape(terms, box_count, parents), (1, 0, 2))
+
     result = pl.pallas_call(
         whole_kernel,
         out_shape=jax.ShapeDtypeStruct((rows, strip_child), f32),
@@ -365,15 +416,15 @@
             pltpu.VMEM((rows, width), bf16),
             pltpu.VMEM((rows, width), bf16),
             pltpu.VMEM((chunks, BAND, 2 * LANES), bf16),
-            pltpu.VMEM((RATIO, WINDOW, 2 * LANES), bf16),
-            pltpu.VMEM((own_boxes, parts, LANES), f32),
+            *[pltpu.VMEM((RATIO, WINDOW, 2 * LANES), bf16)] * 2,
+            *[pltpu.VMEM((own_boxes, parts, LANES), f32)] * 2,
             pltpu.VMEM((chunks, parents, parts, LANES), f32),
             pltpu.VMEM((rounds, box_count * parents, parts, LANES), f32),
-            pltpu.VMEM((2, terms, parts, LANES), f32),
+            pltpu.VMEM((2, 2, terms, parts, LANES), f32),
             pltpu.VMEM((chunks, parents, parts, LANES), f32),
-            pltpu.VMEM((2, parents, parts, LANES), f32),
-            pltpu.VMEM((2, kids, parts, LANES), f32),
-            pltpu.VMEM((rows, LANES), f32),
+            *[pltpu.VMEM((2, parents, parts, LANES), f32)] * 2,
+            *[pltpu.VMEM((2, kids, parts, LANES), f32)] * 2,
+            *[pltpu.VMEM((rows, LANES), f32)] * 2,
             pltpu.VMEM((rows, width), f32),
             pltpu.VMEM((2, rows, LANES), f32),
             pltpu.VMEM((2, rows, LANES), f32),
@@ -385,12 +436,14 @@
             pltpu.SemaphoreType.DMA((rounds,)),
             pltpu.SemaphoreType.DMA((2, 2)),
             pltpu.SemaphoreType.DMA((2, 2)),
-            *[pltpu.VMEM((box_count * parents, parts, LANES), f32)] * rounds,
+            *[pltpu.VMEM((box_count * parents, min(2, rounds - 1 - at), parts, LANES), f32)
+              for at in range(0, rounds - 1, 2)],
+            pltpu.VMEM((box_count * parents, 1, parts, LANES), f32),
         ],
         compiler_params=pltpu.CompilerParams(
             collective_id=0, has_side_effects=True, vmem_limit_bytes=48 * 1024 * 1024),
     )(by_box, jnp.cos(shift_angle), jnp.sin(shift_angle), interp_index, interp_weight, translation,
-      local, slots // kids, slots % kids, interaction_list)
+      local, slots // kids, slots % kids, lists.reshape(-1))
     return jnp.transpose(result.reshape(own_boxes, halves, fields, strip_child), (1, 2, 0, 3))
 
 

time: 64 us -> 50.2 us (0.78)
  the two profiles are of different devices: /device:TPU:1 before, /device:TPU:0 now
where the time goes in v3:
time: 50.2 us; the launch traced here: 49.3 us
  Pallas kernels  40.1 us (80%)
  local copies, waits for them, and re-layouts  9.05 us (18%)
    pallas_call x1, Pallas kernels, shards(): pl.pallas_call(whole_kernel, out_shape=jax.ShapeDtypeStruct((rows, strip_...  40.1 us
    unnamed x9, local copies, waits for them, and re-layouts  3.32 us
    transpose x1, local copies, waits for them, and re-layouts, shards(): by_box = jnp.transpose(child_field, (2, 0, 1, 3)).reshape(rows, strip_child)  2.03 us
    reshape x2, local copies, waits for them, and re-layouts, shards(): result.reshape(own_boxes, halves, fields, strip_child)  1.57 us
    sin x1, local copies, waits for them, and re-layouts, shards(): jnp.sin(shift_angle)  1.4 us

profile of v3, /device:TPU:0, one launch (start us, length us, event | category | flops | bytes accessed | tf_op | source)
XLA Modules:
  0.0 49.3 jit_solution(15744704307414898927)
XLA Ops:
  0.0 0.8 %copy.19 = s32[8,4]{1,0:T(8,128)S(1)} copy(s32[8,4]{0,1:T(4,128)} %param.8) | data formatting | bytes 256 | tf_op args[1]
  0.8 0.1 eq.17
  0.8 0.1 select_reduce_fusion
  1.0 0.8 %copy.20 = s32[27,64]{0,1:T(8,128)S(1)} copy(s32[27,64]{1,0:T(8,128)} %param.12) | data formatting | bytes 13824 | tf_op args[5]
  1.8 0.1 copy.21
  1.9 0.1 reshape.15.list_ref
  2.0 1.4 %fusion = (f32[4,4608]{1,0:T(4,128)S(1)}, f32[4,4608]{1,0:T(4,128)S(1)}) fusion(f32[4,4608]{1,0:T(4,128)} %param.9), kind=kLoop, calls=%fused_computation.9 | loop fusion | bytes 221184 | tf_op jit(solution)/shard_map/sin | solution.py:445
  3.4 2.0 %copy.18 = f32[32,2,4,1152]{3,2,1,0:T(4,128)S(1)} copy(f32[32,2,4,1152]{3,0,2,1:T(8,128)} %bitcast.7) | data formatting | bytes 2359296 | tf_op jit(solution)/shard_map/transpose | solution.py:402
  5.4 0.0 copy-start.2
  5.5 0.4 reshape.13.x_ref
  5.9 0.8 %copy-done.2 = f32[2,27,4608]{2,0,1:T(2,128)S(1)} copy-done((f32[2,27,4608]{2,0,1:T(2,128)S(1)}, f32[2,27,4608]{2,0,1:T(2,128)}, u32[]{:S(2)}) %copy-start.2) | copy-done | bytes 995352
  6.6 0.0 copy-start
  6.7 0.0 copy-start.1
  6.7 0.2 copy.22.table_ref
  6.8 0.7 %copy-done = s32[6,4608]{1,0:T(8,128)S(1)} copy-done((s32[6,4608]{1,0:T(8,128)S(1)}, s32[6,4608]{1,0:T(8,128)}, u32[]{:S(2)}) %copy-start) | copy-done | bytes 110616
  7.6 0.1 copy-done.1
  7.6 40.1 %shard_map.73 = f32[256,1152]{1,0:T(8,128)S(1)} custom-call(f32[256,1152]{1,0:T(8,128)S(1)} %reshape.13.x_ref, f32[4,4608]{1,0:T(4,128)S(1)} %get-tuple-element.6.cos_ref, f32[4,4608]{1,0:T(4,128)S(1)} %get-tuple-element.5.sin_ref, s32[6,4608]{1,0:T(8,128)S(1)} %copy-done, f32[6,4608]{1,0:T(8,128)S(1)} %copy-done.1, f32[2,27,4608]{2,1,0:T(8,128)S(1)} %copy.22.table_ref, ...), custom_call_target="tpu_custom_call" | custom-call | tf_op jit(solution)/shard_map/pallas_call | solution.py:410
  47.7 0.3 reshape.16
  48.1 1.2 %copy.25 = f32[32,2,4,1152]{3,0,2,1:T(8,128)} copy(f32[32,2,4,1152]{3,2,1,0:T(4,128)S(1)} %reshape.16) | data formatting | bytes 2359296 | tf_op jit(solution)/shard_map/reshape | solution.py:447
  (2 shorter events, 0.0 us)
Async XLA Ops:
  5.4 1.2 %copy-start.2 = (f32[2,27,4608]{2,0,1:T(2,128)S(1)}, f32[2,27,4608]{2,0,1:T(2,128)}, u32[]{:S(2)}) copy-start(f32[2,27,4608]{2,0,1:T(2,128)} %param.13) | copy-start | bytes 2985988
  6.6 0.9 %copy-start = (s32[6,4608]{1,0:T(8,128)S(1)}, s32[6,4608]{1,0:T(8,128)}, u32[]{:S(2)}) copy-start(s32[6,4608]{1,0:T(8,128)} %index_ref.1) | copy-start | bytes 331780
  6.7 1.0 %copy-start.1 = (f32[6,4608]{1,0:T(8,128)S(1)}, f32[6,4608]{1,0:T(8,128)}, u32[]{:S(2)}) copy-start(f32[6,4608]{1,0:T(8,128)} %weight_ref.1) | copy-start | bytes 331780
